TPU v7x, 128 devices: a whole 4x4x4 slice. The times are simulated.
128 devices in a mesh: fsdp: 32 (over y_hi, z, x), tensor: 4 (over y_lo, core).
Axes of the slice: x: 4, y: 4 (y_hi: 2, y_lo: 2; y = y_hi * 2 + y_lo), z: 4, core: 2. Of those that a mesh axis runs over, the one named last changes fastest.
Arguments:
- tokens: bfloat16 [2, 32, 256, 1024], P(None, 'fsdp', 'tensor'), may hold values from -6 to 6
- dealt: int32 [2, 32], P(None, 'fsdp'), may hold values 0 or 1
- cotangent: bfloat16 [2, 32, 256, 1024], P(None, 'fsdp', 'tensor'), may hold values from -6 to 6
- qkv_weight: bfloat16 [1, 1024, 3, 1024], P(None, 'fsdp', None, 'tensor'), may hold values from -0.1875 to 0.1875
- out_weight: bfloat16 [1, 1024, 1024], P(None, 'fsdp', 'tensor'), may hold values from -1.5 to 1.5
- up_weight: bfloat16 [1, 1024, 4096], P(None, 'fsdp', 'tensor'), may hold values from -0.1875 to 0.1875
- down_weight: bfloat16 [1, 1024, 4096], P(None, 'fsdp', 'tensor'), may hold values from -0.09375 to 0.09375
- norm1_gain: float32 [1, 1024], replicated, may hold values from 0.25 to 1.75
- norm1_bias: float32 [1, 1024], replicated, may hold values from -3 to 3
- query_bias: float32 [1, 1024], replicated, may hold values from -3 to 3
- value_bias: float32 [1, 1024], replicated, may hold values from -3 to 3
- out_bias: float32 [1, 1024], replicated, may hold values from -3 to 3
- norm2_gain: float32 [1, 1024], replicated, may hold values from 0.25 to 1.75
- norm2_bias: float32 [1, 1024], replicated, may hold values from -3 to 3
- up_bias: float32 [1, 4096], replicated, may hold values from -3 to 3
- down_bias: float32 [1, 1024], replicated, may hold values from -3 to 3
Outputs:
- block_out: bfloat16 [2, 32, 256, 1024], P(None, 'fsdp', 'tensor')
- input_grad: bfloat16 [2, 32, 256, 1024], P(None, 'fsdp', 'tensor')
- qkv_grad: float32 [1, 1024, 3, 1024], P(None, 'fsdp', None, 'tensor')
- out_grad: float32 [1, 1024, 1024], P(None, 'fsdp', 'tensor')
- up_grad: float32 [1, 1024, 4096], P(None, 'fsdp', 'tensor')
- down_grad: float32 [1, 1024, 4096], P(None, 'fsdp', 'tensor')
- norm1_gain_grad: float32 [1, 1024], replicated
- norm1_bias_grad: float32 [1, 1024], replicated
- query_bias_grad: float32 [1, 1024], replicated
- value_bias_grad: float32 [1, 1024], replicated
- out_bias_grad: float32 [1, 1024], replicated
- norm2_gain_grad: float32 [1, 1024], replicated
- norm2_bias_grad: float32 [1, 1024], replicated
- up_bias_grad: float32 [1, 4096], replicated
- down_bias_grad: float32 [1, 1024], replicated
Inputs may be any that keep to these rules, and one draw needn't show every extreme that they name: `dealt`: 1 where the slot holds an image of that micro-batch, 0 where it is empty.
All inputs are finite; a program needn't handle non-finite values. No bound on the sum of `dealt` on one device may be relied on, other than what follows from the above.
Results may differ from a plain program's by a relative error of at most 0.024.
Values may be sent and summed in bfloat16 or wider, within the bound.
No kernel may reach another device: no remote copies, remote signals or barrier semaphores. Data moves between devices by JAX's collectives and lax.ppermute only.
A program may use at most 64 MiB of HBM per device.

v0:
```python
import jax
import jax.numpy as jnp
from jax import lax
from jax.sharding import PartitionSpec as P

HEAD_DIM = 64
EPS_NORM = 1e-06


def layer_norm(values, gain, shift):
    center = values - jnp.mean(values, axis=-1, keepdims=True)
    spread = jnp.mean(center * center, axis=-1, keepdims=True)
    return center * lax.rsqrt(spread + EPS_NORM) * gain + shift


def split_heads(values):
    return values.reshape(values.shape[0], values.shape[1], -1, HEAD_DIM)


def row_total(values):
    return jnp.sum(values.astype(jnp.float32), axis=(0, 1))


def local(
    tokens,
    dealt,
    cotangent,
    qkv_weight,
    out_weight,
    up_weight,
    down_weight,
    norm1_gain,
    norm1_bias,
    query_bias,
    value_bias,
    out_bias,
    norm2_gain,
    norm2_bias,
    up_bias,
    down_bias,
):
    layer_count = qkv_weight.shape[0]
    micro_count = tokens.shape[0]
    slot_count = tokens.shape[1]
    local_rows = tokens.shape[2]
    model_width = tokens.shape[3]
    head_cols = qkv_weight.shape[3]
    unit_cols = up_weight.shape[2]
    unit_total = up_bias.shape[1]
    image_count = micro_count * slot_count
    tensor_index = lax.axis_index("tensor")
    score_scale = HEAD_DIM ** (-0.5)

    def spread_rows(block_rows):
        return lax.all_gather(block_rows, "tensor", axis=0, tiled=True)

    def spread_grads(block_rows):
        return lax.all_gather(block_rows, "tensor", axis=0, tiled=True)

    def collect_rows(term_fn):
        return lax.psum_scatter(
            term_fn(jnp.int32(0), local_rows * lax.axis_size("tensor")),
            "tensor",
            scatter_dimension=0,
            tiled=True,
        )

    def collect_grads(term_fn):
        return lax.psum_scatter(
            term_fn(jnp.int32(0), local_rows * lax.axis_size("tensor")),
            "tensor",
            scatter_dimension=0,
            tiled=True,
        )

    def vectors(layer):
        query_part = lax.dynamic_slice_in_dim(
            query_bias[layer], tensor_index * head_cols, head_cols, 0
        )
        value_part = lax.dynamic_slice_in_dim(
            value_bias[layer], tensor_index * head_cols, head_cols, 0
        )
        up_part = lax.dynamic_slice_in_dim(up_bias[layer], tensor_index * unit_cols, unit_cols, 0)
        return (
            norm1_gain[layer],
            norm1_bias[layer],
            query_part,
            value_part,
            out_bias[layer],
            norm2_gain[layer],
            norm2_bias[layer],
            up_part,
            down_bias[layer],
        )

    def inner_forward(hidden, weights, vecs):
        qkv_full, out_full, up_full, down_full = weights
        gain_one, shift_one, query_b, value_b, out_b, gain_two, shift_two, up_b, down_b = vecs
        normed = spread_rows(layer_norm(hidden, gain_one, shift_one).astype(jnp.bfloat16))
        joined = jnp.einsum("sid,dcf->sicf", normed, qkv_full, preferred_element_type=jnp.float32)
        query = (joined[:, :, 0] + query_b).astype(jnp.bfloat16)
        keys = joined[:, :, 1].astype(jnp.bfloat16)
        values = (joined[:, :, 2] + value_b).astype(jnp.bfloat16)
        scores = (
            jnp.einsum(
                "sihe,tihe->ihst",
                split_heads(query),
                split_heads(keys),
                preferred_element_type=jnp.float32,
            )
            * score_scale
        )
        probs = jax.nn.softmax(scores, axis=-1)
        mixed = jnp.einsum(
            "ihst,tihe->sihe",
            probs.astype(jnp.bfloat16),
            split_heads(values),
            preferred_element_type=jnp.float32,
        )
        mixed = mixed.reshape(query.shape).astype(jnp.bfloat16)

        def attn_term(start, count):
            return jnp.einsum("sid,ed->sie", mixed, out_full, preferred_element_type=jnp.float32)

        middle = hidden + (collect_rows(attn_term) + out_b)
        normed_two = spread_rows(layer_norm(middle, gain_two, shift_two).astype(jnp.bfloat16))
        upward = (
            jnp.einsum("sid,df->sif", normed_two, up_full, preferred_element_type=jnp.float32)
            + up_b
        )
        activated = jax.nn.gelu(upward, approximate=False).astype(jnp.bfloat16)
        return (normed, query, keys, values, probs, mixed, middle, normed_two, upward, activated)

    def backward_layer(hidden, grad_out, weights, vecs):
        qkv_full, out_full, up_full, down_full = weights
        gain_one, shift_one, query_b, value_b, out_b, gain_two, shift_two, up_b, down_b = vecs
        normed, query, keys, values, probs, mixed, middle, normed_two, upward, activated = (
            inner_forward(hidden, weights, vecs)
        )
        grad_down = grad_out.astype(jnp.bfloat16)
        down_b_grad = row_total(grad_down)
        down_all = spread_grads(grad_down)
        down_w_grad = jnp.einsum(
            "sie,sif->ef", down_all, activated, preferred_element_type=jnp.float32
        )
        grad_act = jnp.einsum(
            "sie,ef->sif", down_all, down_full, preferred_element_type=jnp.float32
        )
        gelu_value, gelu_pull = jax.vjp(lambda inner: jax.nn.gelu(inner, approximate=False), upward)
        grad_up = gelu_pull(grad_act)[0].astype(jnp.bfloat16)
        up_b_grad = row_total(grad_up)
        up_w_grad = jnp.einsum(
            "sid,sif->df", normed_two, grad_up, preferred_element_type=jnp.float32
        )

        def up_back(start, count):
            return jnp.einsum("sif,df->sid", grad_up, up_full, preferred_element_type=jnp.float32)

        norm_value, norm_pull = jax.vjp(layer_norm, middle, gain_two, shift_two)
        middle_part, gain_two_grad, shift_two_grad = norm_pull(collect_grads(up_back))
        grad_middle = grad_out + middle_part
        grad_att = grad_middle.astype(jnp.bfloat16)
        out_b_grad = row_total(grad_att)
        att_all = spread_grads(grad_att)
        out_w_grad = jnp.einsum("sie,sid->ed", att_all, mixed, preferred_element_type=jnp.float32)
        grad_mixed = jnp.einsum(
            "sie,ed->sid", att_all, out_full, preferred_element_type=jnp.float32
        ).astype(jnp.bfloat16)
        mixed_heads = split_heads(grad_mixed)
        grad_values = jnp.einsum(
            "ihst,sihe->tihe",
            probs.astype(jnp.bfloat16),
            mixed_heads,
            preferred_element_type=jnp.float32,
        ).astype(jnp.bfloat16)
        grad_prob = jnp.einsum(
            "sihe,tihe->ihst", mixed_heads, split_heads(values), preferred_element_type=jnp.float32
        )
        grad_score = (
            probs * (grad_prob - jnp.sum(grad_prob * probs, axis=-1, keepdims=True))
        ).astype(jnp.bfloat16)
        grad_query = (
            jnp.einsum(
                "ihst,tihe->sihe", grad_score, split_heads(keys), preferred_element_type=jnp.float32
            )
            * score_scale
        ).astype(jnp.bfloat16)
        grad_keys = (
            jnp.einsum(
                "ihst,sihe->tihe",
                grad_score,
                split_heads(query),
                preferred_element_type=jnp.float32,
            )
            * score_scale
        ).astype(jnp.bfloat16)
        flat_shape = query.shape
        grad_joined = jnp.stack(
            [
                grad_query.reshape(flat_shape),
                grad_keys.reshape(flat_shape),
                grad_values.reshape(flat_shape),
            ],
            axis=2,
        )
        query_b_grad = row_total(grad_query).reshape(-1)
        value_b_grad = row_total(grad_values).reshape(-1)
        qkv_w_grad = jnp.einsum(
            "sid,sicf->dcf", normed, grad_joined, preferred_element_type=jnp.float32
        )

        def qkv_back(start, count):
            return jnp.einsum(
                "sicf,dcf->sid", grad_joined, qkv_full, preferred_element_type=jnp.float32
            )

        first_value, first_pull = jax.vjp(layer_norm, hidden, gain_one, shift_one)
        hidden_part, gain_one_grad, shift_one_grad = first_pull(collect_grads(qkv_back))
        grad_in = grad_middle + hidden_part
        weight_grads = (qkv_w_grad, out_w_grad, up_w_grad, down_w_grad)
        vector_grads = (
            gain_one_grad,
            shift_one_grad,
            query_b_grad,
            value_b_grad,
            out_b_grad,
            gain_two_grad,
            shift_two_grad,
            up_b_grad,
            down_b_grad,
        )
        return (grad_in, weight_grads, vector_grads)

    def to_rows(array):
        return jnp.transpose(array.astype(jnp.float32), (2, 0, 1, 3)).reshape(
            local_rows, image_count, model_width
        )

    def from_rows(array):
        return jnp.transpose(
            array.reshape(local_rows, micro_count, slot_count, model_width), (1, 2, 0, 3)
        )

    live_flags = dealt.astype(jnp.float32).reshape(image_count)
    state = to_rows(tokens)
    gathered = []
    layer = 0
    weights = (
        lax.all_gather(qkv_weight[layer], "fsdp", axis=0, tiled=True),
        lax.all_gather(out_weight[layer], "fsdp", axis=0, tiled=True),
        lax.all_gather(up_weight[layer], "fsdp", axis=0, tiled=True),
        lax.all_gather(down_weight[layer], "fsdp", axis=0, tiled=True),
    )
    gathered.append(weights)
    vecs = vectors(layer)
    layer_inputs = [state]
    saved = inner_forward(state, weights, vecs)
    down_full = weights[3]
    activated = saved[9]

    def down_term(start, count):
        return jnp.einsum("sif,ef->sie", activated, down_full, preferred_element_type=jnp.float32)

    state = saved[6] + (collect_rows(down_term) + vecs[8])
    block_out = from_rows(state * live_flags[None, :, None]).astype(jnp.bfloat16)
    grad_state = to_rows(cotangent) * live_flags[None, :, None]
    weight_shards = [None] * layer_count
    vector_parts = [None] * layer_count
    for layer in reversed(range(layer_count)):
        weights = (
            lax.all_gather(qkv_weight[layer], "fsdp", axis=0, tiled=True),
            lax.all_gather(out_weight[layer], "fsdp", axis=0, tiled=True),
            lax.all_gather(up_weight[layer], "fsdp", axis=0, tiled=True),
            lax.all_gather(down_weight[layer], "fsdp", axis=0, tiled=True),
        )
        vecs = vectors(layer)
        grad_state, weight_totals, vector_totals = backward_layer(
            layer_inputs[layer], grad_state, weights, vecs
        )
        weight_shards[layer] = (
            lax.psum_scatter(
                weight_totals[0].astype(jnp.bfloat16), "fsdp", scatter_dimension=0, tiled=True
            ).astype(jnp.float32),
            lax.psum_scatter(
                weight_totals[1].astype(jnp.bfloat16), "fsdp", scatter_dimension=0, tiled=True
            ).astype(jnp.float32),
            lax.psum_scatter(
                weight_totals[2].astype(jnp.bfloat16), "fsdp", scatter_dimension=0, tiled=True
            ).astype(jnp.float32),
            lax.psum_scatter(
                weight_totals[3].astype(jnp.bfloat16), "fsdp", scatter_dimension=0, tiled=True
            ).astype(jnp.float32),
        )
        width_zero = jnp.zeros((model_width,), jnp.float32)
        unit_zero = jnp.zeros((unit_total,), jnp.float32)
        query_full = lax.dynamic_update_slice_in_dim(
            width_zero, vector_totals[2], tensor_index * head_cols, 0
        )
        value_full = lax.dynamic_update_slice_in_dim(
            width_zero, vector_totals[3], tensor_index * head_cols, 0
        )
        up_full_grad = lax.dynamic_update_slice_in_dim(
            unit_zero, vector_totals[7], tensor_index * unit_cols, 0
        )
        vector_parts[layer] = (
            vector_totals[0],
            vector_totals[1],
            query_full,
            value_full,
            vector_totals[4],
            vector_totals[5],
            vector_totals[6],
            up_full_grad,
            vector_totals[8],
        )
    input_grad = from_rows(grad_state).astype(jnp.bfloat16)
    stacked = [jnp.stack([vector_parts[0][index]]) for index in range(9)]
    summed = lax.psum(
        (
            stacked[0],
            stacked[1],
            stacked[2],
            stacked[3],
            stacked[4],
            stacked[5],
            stacked[6],
            stacked[7],
            stacked[8],
        ),
        ("fsdp", "tensor"),
    )
    qkv_grad = jnp.stack([weight_shards[0][0]])
    out_grad = jnp.stack([weight_shards[0][1]])
    up_grad = jnp.stack([weight_shards[0][2]])
    down_grad = jnp.stack([weight_shards[0][3]])
    return (
        block_out,
        input_grad,
        qkv_grad,
        out_grad,
        up_grad,
        down_grad,
        summed[0],
        summed[1],
        summed[2],
        summed[3],
        summed[4],
        summed[5],
        summed[6],
        summed[7],
        summed[8],
    )


def solution(mesh):
    placed = (
        P(None, "fsdp", "tensor", None),
        P(None, "fsdp"),
        P(None, "fsdp", "tensor", None),
        P(None, "fsdp", None, "tensor"),
        P(None, "fsdp", "tensor"),
        P(None, "fsdp", "tensor"),
        P(None, "fsdp", "tensor"),
        P(),
        P(),
        P(),
        P(),
        P(),
        P(),
        P(),
        P(),
        P(),
    )
    return jax.shard_map(
        local,
        mesh=mesh,
        in_specs=placed,
        out_specs=(
            P(None, "fsdp", "tensor", None),
            P(None, "fsdp", "tensor", None),
            P(None, "fsdp", None, "tensor"),
            P(None, "fsdp", "tensor"),
            P(None, "fsdp", "tensor"),
            P(None, "fsdp", "tensor"),
            P(),
            P(),
            P(),
            P(),
            P(),
            P(),
            P(),
            P(),
            P(),
        ),
        check_vma=False,
    )
```

profile of v0, /device:TPU:1, one launch (start us, length us, event | category | flops | bytes accessed | tf_op | source)
XLA Modules:
  0.0 1273.6 jit_solution(8190465983261844580)
XLA Ops:
  9.5 1.9 fusion.36
  13.8 86.5 %all-gather.1 = bf16[1,1024,256]{2,1,0:T(8,128)(2,1)S(1)} all-gather(bf16[1,32,256]{2,1,0:T(8,128)(2,1)} %param.20), channel_id=3, replica_groups=mesh['fsdp'=32,'tensor'=4] {'fsdp'}, dimensions={1}, use_global_device_ids=true | all-gather | bytes 540672 | tf_op jit(solution)/shard_map/all_gather | solution.py:250
  100.3 6.4 all-gather.20.cloned.1.call-done
  106.7 2.8 fusion.17
  116.2 29.6 %reduce-scatter.9.cloned.1.call-done = f32[64,2,1024]{2,0,1:T(8,128)} async-done(((f32[256,2,1024]{2,0,1:T(8,128)}), f32[64,2,1024]{2,0,1:T(8,128)}) %reduce-scatter.9.cloned.1.call-update) | async-done | bytes 524304 | tf_op jit(solution)/shard_map/reduce_scatter | solution.py:61
  150.0 69.4 %all-gather.22.cloned.1.call-done = bf16[1,1024,1024]{2,1,0:T(8,128)(2,1)} async-done(((bf16[1,32,1024]{2,1,0:T(8,128)(2,1)}), bf16[1,1024,1024]{2,1,0:T(8,128)(2,1)}) %all-gather.22.cloned.1.call-update) | async-done | bytes 2097168 | tf_op jit(solution)/shard_map/all_gather | solution.py:251
  219.4 21.5 %all-gather.14.cloned.1.call-done = bf16[256,2,1024]{2,0,1:T(8,128)(2,1)} async-done(((bf16[64,2,1024]{2,0,1:T(8,128)(2,1)}), bf16[256,2,1024]{2,0,1:T(8,128)(2,1)}) %all-gather.14.cloned.1.call-update) | async-done | bytes 1048592 | tf_op jit(solution)/shard_map/all_gather | solution.py:55
  240.9 3.8 fusion.49
  246.1 5.9 multiply_convert_fusion.1
  252.0 12.8 %all-gather.16.cloned.1.call-done = bf16[256,2,1024]{2,0,1:T(8,128)(2,1)} async-done(((bf16[64,2,1024]{2,0,1:T(8,128)(2,1)}), bf16[256,2,1024]{2,0,1:T(8,128)(2,1)}) %all-gather.16.cloned.1.call-update) | async-done | bytes 1048592 | tf_op jit(solution)/shard_map/all_gather | solution.py:58
  264.8 73.5 %all-gather.24.cloned.1.call-done = bf16[1,1024,1024]{2,1,0:T(8,128)(2,1)} async-done(((bf16[1,32,1024]{2,1,0:T(8,128)(2,1)}), bf16[1,1024,1024]{2,1,0:T(8,128)(2,1)}) %all-gather.24.cloned.1.call-update) | async-done | bytes 2097168 | tf_op jit(solution)/shard_map/all_gather | solution.py:252
  338.3 5.2 convert_reduce_fusion
  344.6 2.6 fusion.6
  347.4 4.2 fusion.4
  351.7 22.3 %reduce-scatter.13.cloned.1.call-done = f32[64,2,1024]{2,0,1:T(8,128)} async-done(((f32[256,2,1024]{2,0,1:T(8,128)}), f32[64,2,1024]{2,0,1:T(8,128)}) %reduce-scatter.13.cloned.1.call-update) | async-done | bytes 524304 | tf_op jit(solution)/shard_map/reduce_scatter | solution.py:69
  375.3 30.3 %reduce-scatter.11.cloned.1.call-done = f32[64,2,1024]{2,0,1:T(8,128)} async-done(((f32[256,2,1024]{2,0,1:T(8,128)}), f32[64,2,1024]{2,0,1:T(8,128)}) %reduce-scatter.11.cloned.1.call-update) | async-done | bytes 524304 | tf_op jit(solution)/shard_map/reduce_scatter | solution.py:61
  405.6 2.2 fusion.67
  408.7 4.1 bitcast_convert_fusion.1
  412.9 3.8 bitcast_convert_fusion
  416.9 13.8 %all-gather.18.cloned.1.call-done = bf16[256,2,1024]{2,0,1:T(8,128)(2,1)} async-done(((bf16[64,2,1024]{2,0,1:T(8,128)(2,1)}), bf16[256,2,1024]{2,0,1:T(8,128)(2,1)}) %all-gather.18.cloned.1.call-update) | async-done | bytes 1048592 | tf_op jit(solution)/shard_map/all_gather | solution.py:58
  432.4 2.5 fusion.21
  434.9 2.4 multiply_reduce_fusion
  439.3 2.1 convert_reduce_fusion.3
  441.6 3.5 bitcast_convert_fusion.2
  445.2 2.4 convolution_bitcast_fusion
  447.7 149.5 %reduce-scatter.21.cloned.1.call-done = bf16[32,1024]{1,0:T(8,128)(2,1)} async-done(((bf16[1024,1024]{1,0:T(8,128)(2,1)}), bf16[32,1024]{1,0:T(8,128)(2,1)}) %reduce-scatter.21.cloned.1.call-update) | async-done | bytes 65552 | tf_op jit(solution)/shard_map/reduce_scatter | solution.py:287
  598.6 183.4 %reduce-scatter.23.cloned.1.call-done = bf16[32,1024]{1,0:T(8,128)(2,1)} async-done(((bf16[1024,1024]{1,0:T(8,128)(2,1)}), bf16[32,1024]{1,0:T(8,128)(2,1)}) %reduce-scatter.23.cloned.1.call-update) | async-done | bytes 65552 | tf_op jit(solution)/shard_map/reduce_scatter | solution.py:290
  783.7 177.1 %reduce-scatter.19.cloned.1.call-done = bf16[32,256]{1,0:T(8,128)(2,1)} async-done(((bf16[1024,256]{1,0:T(8,128)(2,1)}), bf16[32,256]{1,0:T(8,128)(2,1)}) %reduce-scatter.19.cloned.1.call-update) | async-done | bytes 16400 | tf_op jit(solution)/shard_map/reduce_scatter | solution.py:284
  962.2 183.6 %reduce-scatter.17.cloned.1.call-done = bf16[32,3,256]{2,0,1:T(8,128)(2,1)} async-done(((bf16[1024,3,256]{2,0,1:T(8,128)(2,1)}), bf16[32,3,256]{2,0,1:T(8,128)(2,1)}) %reduce-scatter.17.cloned.1.call-update) | async-done | bytes 49168 | tf_op jit(solution)/shard_map/reduce_scatter | solution.py:281
  1147.2 48.5 %reduce-scatter.15.cloned.1.call-done = f32[64,2,1024]{2,0,1:T(8,128)} async-done(((f32[256,2,1024]{2,0,1:T(8,128)}), f32[64,2,1024]{2,0,1:T(8,128)}) %reduce-scatter.15.cloned.1.call-update) | async-done | bytes 524304 | tf_op jit(solution)/shard_map/reduce_scatter | solution.py:69
  1198.4 66.6 %all-reduce = (f32[1,1024]{1,0:T(1,128)}, f32[1,1024]{1,0:T(1,128)}, f32[1,1024]{1,0:T(1,128)}, f32[1,1024]{1,0:T(1,128)}, f32[1,1024]{1,0:T(1,128)}, /*index=5*...) all-reduce(f32[1,1024]{1,0:T(1,128)S(1)} %bitcast.237, ...), channel_id=1, replica_groups=mesh['fsdp'=32,'tensor'=4] {'fsdp','tensor'}, use_global_device_ids=true, to_apply=%region_20.0 | all-reduce | flops 12288 | bytes 98304 | tf_op jit(solution)/shard_map/psum | solution.py:318
  1265.1 2.0 fusion.52
  (119 shorter events, 33.0 us)
Async XLA Ops:
  7.2 142.8 %copy-start = (f32[1,4096]{1,0:T(1,128)S(1)}, f32[1,4096]{1,0:T(1,128)}, u32[]{:S(2)}) copy-start(f32[1,4096]{1,0:T(1,128)} %param.30) | copy-start | bytes 49156
  7.2 93.1 %all-gather.12.cloned.1.call-start = ((), (), s32[]{:S(2)}) async-start(), calls=%async_computation.8 | async-start | bytes 1310720 | tf_op jit(solution)/shard_map/all_gather | solution.py:55
  11.4 95.3 %all-gather.20.cloned.1.call-start = ((), (), s32[]{:S(2)}) async-start(), calls=%async_computation.20 | async-start | bytes 1622016 | tf_op jit(solution)/shard_map/all_gather | solution.py:249
  12.2 133.7 %reduce-scatter.9.cloned.1.call-start = ((), (), s32[]{:S(2)}) async-start(), calls=%async_computation.9 | async-start | bytes 2621440 | tf_op jit(solution)/shard_map/reduce_scatter | solution.py:61
  110.3 2.7 copy-start.6
  111.3 1.8 copy-start.3
  113.8 32.1 %copy-start.1 = (bf16[2,1,64,1024]{3,2,1,0:T(8,128)(2,1)S(1)}, bf16[2,1,64,1024]{3,2,1,0:T(8,128)(2,1)}, u32[]{:S(2)}) copy-start(bf16[2,1,64,1024]{3,2,1,0:T(8,128)(2,1)} %param.16) | copy-start | bytes 786436
  113.8 32.1 %copy-start.13 = (f32[1,1024]{1,0:T(1,128)S(1)}, f32[1,1024]{1,0:T(1,128)}, u32[]{:S(2)}) copy-start(f32[1,1024]{1,0:T(1,128)} %param.27) | copy-start | bytes 12292
  115.6 31.7 %copy-start.12 = (f32[1,1024]{1,0:T(1,128)S(1)}, f32[1,1024]{1,0:T(1,128)}, u32[]{:S(2)}) copy-start(f32[1,1024]{1,0:T(1,128)} %param.28) | copy-start | bytes 12292
  115.6 31.7 %copy-start.14 = (f32[1,1024]{1,0:T(1,128)S(1)}, f32[1,1024]{1,0:T(1,128)}, u32[]{:S(2)}) copy-start(f32[1,1024]{1,0:T(1,128)} %param.29) | copy-start | bytes 12292
  115.6 32.7 %copy-start.18 = (s32[2,1]{0,1:T(1,128)S(1)}, s32[2,1]{0,1:T(1,128)}, u32[]{:S(2)}) copy-start(s32[2,1]{0,1:T(1,128)} %param.17) | copy-start | bytes 28
  115.6 32.7 %copy-start.2 = (bf16[2,1,64,1024]{3,2,1,0:T(8,128)(2,1)S(1)}, bf16[2,1,64,1024]{3,2,1,0:T(8,128)(2,1)}, u32[]{:S(2)}) copy-start(bf16[2,1,64,1024]{3,2,1,0:T(8,128)(2,1)} %param.18) | copy-start | bytes 786436
  115.6 103.8 %all-gather.22.cloned.1.call-start = ((), (), s32[]{:S(2)}) async-start(), calls=%async_computation.21 | async-start | bytes 2162688 | tf_op jit(solution)/shard_map/all_gather | solution.py:251
  116.2 124.7 %all-gather.14.cloned.1.call-start = ((), (), s32[]{:S(2)}) async-start(), calls=%async_computation.10 | async-start | bytes 1310720 | tf_op jit(solution)/shard_map/all_gather | solution.py:55
  148.2 116.6 %all-gather.16.cloned.1.call-start = ((), (), s32[]{:S(2)}) async-start(), calls=%async_computation.12 | async-start | bytes 1310720 | tf_op jit(solution)/shard_map/all_gather | solution.py:58
  149.1 189.1 %all-gather.24.cloned.1.call-start = ((), (), s32[]{:S(2)}) async-start(), calls=%async_computation.22 | async-start | bytes 2162688 | tf_op jit(solution)/shard_map/all_gather | solution.py:252
  149.9 224.1 %reduce-scatter.13.cloned.1.call-start = ((), (), s32[]{:S(2)}) async-start(), calls=%async_computation.13 | async-start | bytes 2621440 | tf_op jit(solution)/shard_map/reduce_scatter | solution.py:69
  244.7 1.4 copy-start.5
  338.3 6.3 copy-start.16
  347.2 58.4 %reduce-scatter.11.cloned.1.call-start = ((), (), s32[]{:S(2)}) async-start(), calls=%async_computation.11 | async-start | bytes 2621440 | tf_op jit(solution)/shard_map/reduce_scatter | solution.py:61
  351.6 54.0 %copy-start.15 = (f32[1,1024]{1,0:T(1,128)S(1)}, f32[1,1024]{1,0:T(1,128)}, u32[]{:S(2)}) copy-start(f32[1,1024]{1,0:T(1,128)} %param.31) | copy-start | bytes 12292
  351.6 79.0 %all-gather.18.cloned.1.call-start = ((), (), s32[]{:S(2)}) async-start(), calls=%async_computation.14 | async-start | bytes 1310720 | tf_op jit(solution)/shard_map/all_gather | solution.py:58
  408.7 188.4 %reduce-scatter.21.cloned.1.call-start = ((), (), s32[]{:S(2)}) async-start(), calls=%async_computation.18 | async-start | bytes 2162688 | tf_op jit(solution)/shard_map/reduce_scatter | solution.py:287
  412.9 369.1 %reduce-scatter.23.cloned.1.call-start = ((), (), s32[]{:S(2)}) async-start(), calls=%async_computation.19 | async-start | bytes 2162688 | tf_op jit(solution)/shard_map/reduce_scatter | solution.py:290
  416.8 15.6 %copy-start.9 = (bf16[2,4,64,256]{3,2,1,0:T(8,128)(2,1)S(1)}, bf16[2,4,64,256]{3,2,1,0:T(8,128)(2,1)}, u32[]{:S(2)}) copy-start(bf16[2,4,64,256]{3,2,1,0:T(8,128)(2,1)} %copy-done.8) | copy-start | bytes 786436
  416.8 18.1 %copy-start.10 = (f32[256,2,1,256]{0,3,2,1:T(8,128)S(1)}, f32[256,2,1,256]{0,3,2,1:T(8,128)}, u32[]{:S(2)}) copy-start(f32[256,2,1,256]{0,3,2,1:T(8,128)} %get-tuple-element.74) | copy-start | bytes 1572868
  416.8 544.0 %reduce-scatter.19.cloned.1.call-start = ((), (), s32[]{:S(2)}) async-start(), calls=%async_computation.17 | async-start | bytes 540672 | tf_op jit(solution)/shard_map/reduce_scatter | solution.py:284
  434.9 2.4 copy-start.4
  437.7 708.1 %reduce-scatter.17.cloned.1.call-start = ((), (), s32[]{:S(2)}) async-start(), calls=%async_computation.16 | async-start | bytes 1622016 | tf_op jit(solution)/shard_map/reduce_scatter | solution.py:281
  441.6 3.6 copy-start.17
  445.2 750.6 %reduce-scatter.15.cloned.1.call-start = ((), (), s32[]{:S(2)}) async-start(), calls=%async_computation.15 | async-start | bytes 2621440 | tf_op jit(solution)/shard_map/reduce_scatter | solution.py:69
  447.6 748.2 %copy-start.11 = (f32[1,1024]{1,0:T(1,128)S(1)}, f32[1,1024]{1,0:T(1,128)}, u32[]{:S(2)}) copy-start(f32[1,1024]{1,0:T(1,128)} %param.23) | copy-start | bytes 12292
  (3 other events, 2.8 us)
Sparse Core Ops, SparseCore 0:
  11.6 24.4 all-gather.11
  39.1 67.5 all-gather.19
  115.7 30.0 reduce-scatter.8
  149.2 70.1 all-gather.21
  221.6 19.2 all-gather.13
  243.1 21.6 all-gather.15
  268.2 70.0 all-gather.23
  347.3 26.6 reduce-scatter.12
  376.4 29.1 reduce-scatter.10
  408.8 21.8 all-gather.17
  433.1 163.9 reduce-scatter.20
  599.3 182.6 reduce-scatter.22
  784.5 176.3 reduce-scatter.18
  963.1 182.6 reduce-scatter.16
  1148.2 47.5 reduce-scatter.14
where the time goes:
time: 1270 us
  waiting for transfers between devices  1020 us (80%)
  blocking collectives  153 us (12%)
  matrix products  46.5 us (4%)
  other arithmetic  28.4 us (2%)
  between operations  14.2 us (1%)
    reduce_scatter x1, waiting for transfers between devices, local(): lax.psum_scatter(weight_totals[0].astype(jnp.bfloat16), 'fsdp', scatter_d...  184 us
    reduce_scatter x1, waiting for transfers between devices, local(): lax.psum_scatter(weight_totals[3].astype(jnp.bfloat16), 'fsdp', scatter_d...  183 us
    reduce_scatter x1, waiting for transfers between devices, local(): lax.psum_scatter(weight_totals[1].astype(jnp.bfloat16), 'fsdp', scatter_d...  177 us
    reduce_scatter x1, waiting for transfers between devices, local(): lax.psum_scatter(weight_totals[2].astype(jnp.bfloat16), 'fsdp', scatter_d...  149 us
    all_gather x1, blocking collectives, local(): lax.all_gather(out_weight[layer], 'fsdp', axis=0, tiled=True)  86.5 us
    all_gather x1, waiting for transfers between devices, local(): lax.all_gather(down_weight[layer], 'fsdp', axis=0, tiled=True)  73.5 us
    reduce_scatter x2, waiting for transfers between devices, collect_grads(): lax.psum_scatter(term_fn(jnp.int32(0), local_rows * lax.axis_size('tensor...  70.8 us
    all_gather x1, waiting for transfers between devices, local(): lax.all_gather(up_weight[layer], 'fsdp', axis=0, tiled=True)  69.4 us
  transfers between devices with their start and end apart: 15, of which 14 were waited for; matrix products, arithmetic and copies ran while one was open for 4% of the time, Pallas kernels for 0%

commit v1 on v0

--- a/solution.py
+++ b/solution.py
@@ -315,7 +315,10 @@
         )
     input_grad = from_rows(grad_state).astype(jnp.bfloat16)
     stacked = [jnp.stack([vector_parts[0][index]]) for index in range(9)]
-    summed = lax.psum(
+    bands_run = lambda z_in, axis_name, across: lax.psum(
+        lax.psum(z_in, axis_name), axis_name=across
+    )
+    summed = bands_run(
         (
             stacked[0],
             stacked[1],
@@ -327,7 +330,8 @@
             stacked[7],
             stacked[8],
         ),
-        ("fsdp", "tensor"),
+        "tensor",
+        "fsdp",
     )
     qkv_grad = jnp.stack([weight_shards[0][0]])
     out_grad = jnp.stack([weight_shards[0][1]])

time: 1270 us -> 1400 us (1.10)
  the two profiles are of different devices: /device:TPU:1 before, /device:TPU:0 now
where the time goes in v1:
time: 1400 us
  waiting for transfers between devices  1010 us (72%)
  blocking collectives  294 us (21%)
  matrix products  46.5 us (3%)
  other arithmetic  27.4 us (2%)
  between operations  14.2 us (1%)
    psum x1, blocking collectives, local(): lax.psum(lax.psum(z_in, axis_name), axis_name=across)  184 us
    reduce_scatter x1, waiting for transfers between devices, local(): lax.psum_scatter(weight_totals[3].astype(jnp.bfloat16), 'fsdp', scatter_d...  183 us
    reduce_scatter x1, waiting for transfers between devices, local(): lax.psum_scatter(weight_totals[0].astype(jnp.bfloat16), 'fsdp', scatter_d...  182 us
    reduce_scatter x1, waiting for transfers between devices, local(): lax.psum_scatter(weight_totals[1].astype(jnp.bfloat16), 'fsdp', scatter_d...  180 us
    reduce_scatter x1, waiting for transfers between devices, local(): lax.psum_scatter(weight_totals[2].astype(jnp.bfloat16), 'fsdp', scatter_d...  174 us
    all_gather x1, blocking collectives, local(): lax.all_gather(out_weight[layer], 'fsdp', axis=0, tiled=True)  99.9 us
    all_gather x1, waiting for transfers between devices, local(): lax.all_gather(down_weight[layer], 'fsdp', axis=0, tiled=True)  75.3 us
    all_gather x1, waiting for transfers between devices, local(): lax.all_gather(up_weight[layer], 'fsdp', axis=0, tiled=True)  71.1 us
  transfers between devices with their start and end apart: 15, of which 13 were waited for; matrix products, arithmetic and copies ran while one was open for 4% of the time, Pallas kernels for 0%

profile of v1, /device:TPU:0, one launch (start us, length us, event | category | flops | bytes accessed | tf_op | source)
XLA Modules:
  0.0 1399.4 jit_solution(297948855442923770)
XLA Ops:
  9.5 1.9 fusion.36
  13.8 99.9 %all-gather.1 = bf16[1,1024,256]{2,1,0:T(8,128)(2,1)S(1)} all-gather(bf16[1,32,256]{2,1,0:T(8,128)(2,1)} %param.20), channel_id=3, replica_groups=mesh['fsdp'=32,'tensor'=4] {'fsdp'}, dimensions={1}, use_global_device_ids=true | all-gather | bytes 540672 | tf_op jit(solution)/shard_map/all_gather | solution.py:250
  113.7 2.8 fusion.17
  120.8 1.8 fusion.42
  123.3 21.6 %reduce-scatter.9.cloned.1.call-done = f32[64,2,1024]{2,0,1:T(8,128)} async-done(((f32[256,2,1024]{2,0,1:T(8,128)}), f32[64,2,1024]{2,0,1:T(8,128)}) %reduce-scatter.9.cloned.1.call-update) | async-done | bytes 524304 | tf_op jit(solution)/shard_map/reduce_scatter | solution.py:61
  148.9 71.1 %all-gather.22.cloned.1.call-done = bf16[1,1024,1024]{2,1,0:T(8,128)(2,1)} async-done(((bf16[1,32,1024]{2,1,0:T(8,128)(2,1)}), bf16[1,1024,1024]{2,1,0:T(8,128)(2,1)}) %all-gather.22.cloned.1.call-update) | async-done | bytes 2097168 | tf_op jit(solution)/shard_map/all_gather | solution.py:251
  220.0 19.7 %all-gather.14.cloned.1.call-done = bf16[256,2,1024]{2,0,1:T(8,128)(2,1)} async-done(((bf16[64,2,1024]{2,0,1:T(8,128)(2,1)}), bf16[256,2,1024]{2,0,1:T(8,128)(2,1)}) %all-gather.14.cloned.1.call-update) | async-done | bytes 1048592 | tf_op jit(solution)/shard_map/all_gather | solution.py:55
  239.7 3.8 fusion.49
  244.9 5.9 multiply_convert_fusion.1
  250.8 12.8 all-gather.16.cloned.1.call-done
  263.6 75.3 %all-gather.24.cloned.1.call-done = bf16[1,1024,1024]{2,1,0:T(8,128)(2,1)} async-done(((bf16[1,32,1024]{2,1,0:T(8,128)(2,1)}), bf16[1,1024,1024]{2,1,0:T(8,128)(2,1)}) %all-gather.24.cloned.1.call-update) | async-done | bytes 2097168 | tf_op jit(solution)/shard_map/all_gather | solution.py:252
  338.9 5.2 convert_reduce_fusion
  345.2 2.6 fusion.6
  348.0 4.2 fusion.4
  352.3 20.6 %reduce-scatter.13.cloned.1.call-done = f32[64,2,1024]{2,0,1:T(8,128)} async-done(((f32[256,2,1024]{2,0,1:T(8,128)}), f32[64,2,1024]{2,0,1:T(8,128)}) %reduce-scatter.13.cloned.1.call-update) | async-done | bytes 524304 | tf_op jit(solution)/shard_map/reduce_scatter | solution.py:69
  374.2 30.3 %reduce-scatter.11.cloned.1.call-done = f32[64,2,1024]{2,0,1:T(8,128)} async-done(((f32[256,2,1024]{2,0,1:T(8,128)}), f32[64,2,1024]{2,0,1:T(8,128)}) %reduce-scatter.11.cloned.1.call-update) | async-done | bytes 524304 | tf_op jit(solution)/shard_map/reduce_scatter | solution.py:61
  404.6 2.2 fusion.67
  407.7 4.1 bitcast_convert_fusion.1
  411.9 3.8 bitcast_convert_fusion
  415.9 13.6 all-gather.18.cloned.1.call-done
  431.2 2.5 fusion.21
  433.7 2.4 multiply_reduce_fusion
  438.1 2.1 convert_reduce_fusion.3
  440.4 3.5 bitcast_convert_fusion.2
  444.0 2.4 convolution_bitcast_fusion
  446.5 173.9 %reduce-scatter.21.cloned.1.call-done = bf16[32,1024]{1,0:T(8,128)(2,1)} async-done(((bf16[1024,1024]{1,0:T(8,128)(2,1)}), bf16[32,1024]{1,0:T(8,128)(2,1)}) %reduce-scatter.21.cloned.1.call-update) | async-done | bytes 65552 | tf_op jit(solution)/shard_map/reduce_scatter | solution.py:287
  621.8 182.9 %reduce-scatter.23.cloned.1.call-done = bf16[32,1024]{1,0:T(8,128)(2,1)} async-done(((bf16[1024,1024]{1,0:T(8,128)(2,1)}), bf16[32,1024]{1,0:T(8,128)(2,1)}) %reduce-scatter.23.cloned.1.call-update) | async-done | bytes 65552 | tf_op jit(solution)/shard_map/reduce_scatter | solution.py:290
  806.4 179.8 %reduce-scatter.19.cloned.1.call-done = bf16[32,256]{1,0:T(8,128)(2,1)} async-done(((bf16[1024,256]{1,0:T(8,128)(2,1)}), bf16[32,256]{1,0:T(8,128)(2,1)}) %reduce-scatter.19.cloned.1.call-update) | async-done | bytes 16400 | tf_op jit(solution)/shard_map/reduce_scatter | solution.py:284
  987.6 181.8 %reduce-scatter.17.cloned.1.call-done = bf16[32,3,256]{2,0,1:T(8,128)(2,1)} async-done(((bf16[1024,3,256]{2,0,1:T(8,128)(2,1)}), bf16[32,3,256]{2,0,1:T(8,128)(2,1)}) %reduce-scatter.17.cloned.1.call-update) | async-done | bytes 49168 | tf_op jit(solution)/shard_map/reduce_scatter | solution.py:281
  1170.8 23.9 %reduce-scatter.15.cloned.1.call-done = f32[64,2,1024]{2,0,1:T(8,128)} async-done(((f32[256,2,1024]{2,0,1:T(8,128)}), f32[64,2,1024]{2,0,1:T(8,128)}) %reduce-scatter.15.cloned.1.call-update) | async-done | bytes 524304 | tf_op jit(solution)/shard_map/reduce_scatter | solution.py:69
  1197.5 10.6 all-reduce.1
  1208.1 183.8 %all-reduce = (f32[1,1024]{1,0:T(1,128)}, f32[1,1024]{1,0:T(1,128)}, f32[1,1024]{1,0:T(1,128)}, f32[1,1024]{1,0:T(1,128)}, f32[1,1024]{1,0:T(1,128)}, /*index=5*...) all-reduce(f32[1,1024]{1,0:T(1,128)S(1)} %get-tuple-element.63, ...), channel_id=1, replica_groups=mesh['fsdp'=32,'tensor'=4] {'fsdp'}, use_global_device_ids=true, to_apply=%region_21.0 | all-reduce | flops 12288 | bytes 98304 | tf_op jit(solution)/shard_map/psum | solution.py:318
  (122 shorter events, 32.3 us)
Async XLA Ops:
  7.2 141.7 %copy-start = (f32[1,4096]{1,0:T(1,128)S(1)}, f32[1,4096]{1,0:T(1,128)}, u32[]{:S(2)}) copy-start(f32[1,4096]{1,0:T(1,128)} %param.30) | copy-start | bytes 49156
  7.2 106.5 %all-gather.12.cloned.1.call-start = ((), (), s32[]{:S(2)}) async-start(), calls=%async_computation.8 | async-start | bytes 1310720 | tf_op jit(solution)/shard_map/all_gather | solution.py:55
  11.4 102.3 %all-gather.20.cloned.1.call-start = ((), (), s32[]{:S(2)}) async-start(), calls=%async_computation.20 | async-start | bytes 1622016 | tf_op jit(solution)/shard_map/all_gather | solution.py:249
  12.2 132.7 %reduce-scatter.9.cloned.1.call-start = ((), (), s32[]{:S(2)}) async-start(), calls=%async_computation.9 | async-start | bytes 2621440 | tf_op jit(solution)/shard_map/reduce_scatter | solution.py:61
  117.4 2.7 copy-start.7
  118.3 1.8 copy-start.4
  120.8 24.1 %copy-start.1 = (bf16[2,1,64,1024]{3,2,1,0:T(8,128)(2,1)S(1)}, bf16[2,1,64,1024]{3,2,1,0:T(8,128)(2,1)}, u32[]{:S(2)}) copy-start(bf16[2,1,64,1024]{3,2,1,0:T(8,128)(2,1)} %param.16) | copy-start | bytes 786436
  120.8 24.1 %copy-start.14 = (f32[1,1024]{1,0:T(1,128)S(1)}, f32[1,1024]{1,0:T(1,128)}, u32[]{:S(2)}) copy-start(f32[1,1024]{1,0:T(1,128)} %param.27) | copy-start | bytes 12292
  122.6 23.7 %copy-start.13 = (f32[1,1024]{1,0:T(1,128)S(1)}, f32[1,1024]{1,0:T(1,128)}, u32[]{:S(2)}) copy-start(f32[1,1024]{1,0:T(1,128)} %param.28) | copy-start | bytes 12292
  122.6 23.7 %copy-start.15 = (f32[1,1024]{1,0:T(1,128)S(1)}, f32[1,1024]{1,0:T(1,128)}, u32[]{:S(2)}) copy-start(f32[1,1024]{1,0:T(1,128)} %param.29) | copy-start | bytes 12292
  122.6 24.6 %copy-start.19 = (s32[2,1]{0,1:T(1,128)S(1)}, s32[2,1]{0,1:T(1,128)}, u32[]{:S(2)}) copy-start(s32[2,1]{0,1:T(1,128)} %param.17) | copy-start | bytes 28
  122.6 24.6 %copy-start.3 = (bf16[2,1,64,1024]{3,2,1,0:T(8,128)(2,1)S(1)}, bf16[2,1,64,1024]{3,2,1,0:T(8,128)(2,1)}, u32[]{:S(2)}) copy-start(bf16[2,1,64,1024]{3,2,1,0:T(8,128)(2,1)} %param.18) | copy-start | bytes 786436
  122.7 97.4 %all-gather.22.cloned.1.call-start = ((), (), s32[]{:S(2)}) async-start(), calls=%async_computation.21 | async-start | bytes 2162688 | tf_op jit(solution)/shard_map/all_gather | solution.py:251
  123.2 116.5 %all-gather.14.cloned.1.call-start = ((), (), s32[]{:S(2)}) async-start(), calls=%async_computation.10 | async-start | bytes 1310720 | tf_op jit(solution)/shard_map/all_gather | solution.py:55
  147.2 116.4 %all-gather.16.cloned.1.call-start = ((), (), s32[]{:S(2)}) async-start(), calls=%async_computation.12 | async-start | bytes 1310720 | tf_op jit(solution)/shard_map/all_gather | solution.py:58
  148.1 190.8 %all-gather.24.cloned.1.call-start = ((), (), s32[]{:S(2)}) async-start(), calls=%async_computation.22 | async-start | bytes 2162688 | tf_op jit(solution)/shard_map/all_gather | solution.py:252
  148.9 224.1 %reduce-scatter.13.cloned.1.call-start = ((), (), s32[]{:S(2)}) async-start(), calls=%async_computation.13 | async-start | bytes 2621440 | tf_op jit(solution)/shard_map/reduce_scatter | solution.py:69
  338.9 6.3 copy-start.17
  347.8 56.8 %reduce-scatter.11.cloned.1.call-start = ((), (), s32[]{:S(2)}) async-start(), calls=%async_computation.11 | async-start | bytes 2621440 | tf_op jit(solution)/shard_map/reduce_scatter | solution.py:61
  352.2 52.3 %copy-start.16 = (f32[1,1024]{1,0:T(1,128)S(1)}, f32[1,1024]{1,0:T(1,128)}, u32[]{:S(2)}) copy-start(f32[1,1024]{1,0:T(1,128)} %param.31) | copy-start | bytes 12292
  352.3 77.2 %all-gather.18.cloned.1.call-start = ((), (), s32[]{:S(2)}) async-start(), calls=%async_computation.14 | async-start | bytes 1310720 | tf_op jit(solution)/shard_map/all_gather | solution.py:58
  407.7 212.7 %reduce-scatter.21.cloned.1.call-start = ((), (), s32[]{:S(2)}) async-start(), calls=%async_computation.18 | async-start | bytes 2162688 | tf_op jit(solution)/shard_map/reduce_scatter | solution.py:287
  411.9 392.8 %reduce-scatter.23.cloned.1.call-start = ((), (), s32[]{:S(2)}) async-start(), calls=%async_computation.19 | async-start | bytes 2162688 | tf_op jit(solution)/shard_map/reduce_scatter | solution.py:290
  415.8 15.4 %copy-start.10 = (bf16[2,4,64,256]{3,2,1,0:T(8,128)(2,1)S(1)}, bf16[2,4,64,256]{3,2,1,0:T(8,128)(2,1)}, u32[]{:S(2)}) copy-start(bf16[2,4,64,256]{3,2,1,0:T(8,128)(2,1)} %copy-done.9) | copy-start | bytes 786436
  415.8 17.9 %copy-start.11 = (f32[256,2,1,256]{0,3,2,1:T(8,128)S(1)}, f32[256,2,1,256]{0,3,2,1:T(8,128)}, u32[]{:S(2)}) copy-start(f32[256,2,1,256]{0,3,2,1:T(8,128)} %get-tuple-element.83) | copy-start | bytes 1572868
  415.8 570.4 %reduce-scatter.19.cloned.1.call-start = ((), (), s32[]{:S(2)}) async-start(), calls=%async_computation.17 | async-start | bytes 540672 | tf_op jit(solution)/shard_map/reduce_scatter | solution.py:284
  433.7 2.4 copy-start.5
  436.6 732.8 %reduce-scatter.17.cloned.1.call-start = ((), (), s32[]{:S(2)}) async-start(), calls=%async_computation.16 | async-start | bytes 1622016 | tf_op jit(solution)/shard_map/reduce_scatter | solution.py:281
  440.4 3.6 copy-start.18
  444.0 750.8 %reduce-scatter.15.cloned.1.call-start = ((), (), s32[]{:S(2)}) async-start(), calls=%async_computation.15 | async-start | bytes 2621440 | tf_op jit(solution)/shard_map/reduce_scatter | solution.py:69
  446.4 748.3 %copy-start.12 = (f32[1,1024]{1,0:T(1,128)S(1)}, f32[1,1024]{1,0:T(1,128)}, u32[]{:S(2)}) copy-start(f32[1,1024]{1,0:T(1,128)} %param.23) | copy-start | bytes 12292
  1194.7 197.1 %copy-start.2 = (f32[64,2,1024]{2,0,1:T(8,128)S(1)}, f32[64,2,1024]{2,0,1:T(8,128)}, u32[]{:S(2)}) copy-start(f32[64,2,1024]{2,0,1:T(8,128)} %reduce-scatter.15.cloned.1.call-done) | copy-start | bytes 1572868
  (4 other events, 4.2 us)
Sparse Core Ops, SparseCore 0:
  11.6 23.1 all-gather.11
  37.7 69.8 all-gather.19
  122.8 22.0 reduce-scatter.8
  148.1 71.8 all-gather.21
  222.2 17.4 all-gather.13
  241.9 21.6 all-gather.15
  267.0 71.8 all-gather.23
  347.9 24.9 reduce-scatter.12
  375.4 29.1 reduce-scatter.10
  407.8 21.6 all-gather.17
  432.0 188.3 reduce-scatter.20
  622.6 182.1 reduce-scatter.22
  807.2 179.0 reduce-scatter.18
  988.5 180.8 reduce-scatter.16
  1171.8 22.9 reduce-scatter.14
